TPU v7x, 32 devices: a whole 2x2x4 slice. The times are simulated.
32 devices in a mesh: groups: 2 (over y), tensor: 16 (over z, x, core).
Axes of the slice: x: 2, y: 2, z: 4, core: 2. Of those that a mesh axis runs over, the one named last changes fastest.
Arguments:
- tokens: bfloat16 [64, 8192], P(('groups', 'tensor')), parts along dimension 0, may hold values from -6 to 6
- norm_gain: float32 [8192], replicated, may hold values from 0.1 to 1.9
- token_order: int32 [64], P('groups'), parts along dimension 0, may hold values from 0 to 31, each once
- gate_weight: bfloat16 [8192, 16384], P(None, 'tensor'), may hold values from -0.09375 to 0.09375
- gate_keep: int32 [128, 256], P(None, 'tensor'), may hold values 0 or 1
- gate_expo: int32 [128, 256], P(None, 'tensor'), may hold values from -1 to 1
- up_weight: bfloat16 [8192, 16384], P(None, 'tensor'), may hold values from -0.09375 to 0.09375
- up_keep: int32 [128, 256], P(None, 'tensor'), may hold values 0 or 1
- up_expo: int32 [128, 256], P(None, 'tensor'), may hold values from -1 to 1
- down_weight: bfloat16 [16384, 8192], P('tensor'), may hold values from -0.0625 to 0.0625
- down_keep: int32 [256, 128], P('tensor'), may hold values 0 or 1
- down_expo: int32 [256, 128], P('tensor'), may hold values from -1 to 1
Outputs:
- ffn_out: bfloat16 [64, 8192], P(('groups', 'tensor')), parts along dimension 0
There are 2 independent parts, one for each index of `groups`. A program takes and returns all parts, laid end to end along the dimension named above; an argument that names none is the same for every part. Nothing has to cross between parts.
Inputs may be any that keep to these rules, and one draw needn't show every extreme that they name: `token_order`: each token appears exactly once.
All inputs are finite; a program needn't handle non-finite values. No bound on the sum of `gate_keep` or of `up_keep` or of `down_keep` on one device may be relied on, other than what follows from the above.
Results may differ from a plain program's by a relative error of at most 0.0065.
Values may be sent and summed in bfloat16 or wider, within the bound.
A program may use at most 128 MiB of HBM per device.

v0:
```python
import jax
import jax.numpy as jnp
from jax import lax
from jax.sharding import PartitionSpec as P


def scaled(weight, keep, expo):
    rows, cols = weight.shape
    brow, bcol = keep.shape
    factor = jnp.where(keep > 0, jnp.exp2(expo.astype(jnp.float32)), 0.0).astype(jnp.bfloat16)
    widened = jnp.repeat(factor, cols // bcol, axis=1)
    blocks = weight.reshape(brow, rows // brow, cols) * widened[:, None, :]
    return blocks.reshape(rows, cols)


def normalize(tokens, norm_gain):
    values = tokens.astype(jnp.float32)
    meansq = jnp.mean(values * values, axis=-1, keepdims=True)
    return (values * lax.rsqrt(meansq + 1e-05) * norm_gain).astype(jnp.bfloat16)


def body(
    tokens,
    norm_gain,
    token_order,
    gate_weight,
    gate_keep,
    gate_expo,
    up_weight,
    up_keep,
    up_expo,
    down_weight,
    down_keep,
    down_expo,
):
    normed = normalize(tokens, norm_gain)
    gate_scaled = scaled(gate_weight, gate_keep, gate_expo)
    up_scaled = scaled(up_weight, up_keep, up_expo)
    down_scaled = scaled(down_weight, down_keep, down_expo)
    everything = lax.all_gather(normed, "tensor", axis=0, tiled=True)
    gate = jnp.dot(everything, gate_scaled, preferred_element_type=jnp.float32)
    up = jnp.dot(everything, up_scaled, preferred_element_type=jnp.float32)
    hidden = (jax.nn.silu(gate) * up).astype(jnp.bfloat16)
    terms = jnp.dot(hidden[token_order], down_scaled, preferred_element_type=jnp.float32)
    summed = lax.psum_scatter(terms, "tensor", scatter_dimension=0, tiled=True)
    return summed.astype(jnp.bfloat16)


def solution(mesh):
    return jax.shard_map(
        body,
        mesh=mesh,
        in_specs=(
            P(("groups", "tensor"), None),
            P(),
            P("groups"),
            P(None, "tensor"),
            P(None, "tensor"),
            P(None, "tensor"),
            P(None, "tensor"),
            P(None, "tensor"),
            P(None, "tensor"),
            P("tensor", None),
            P("tensor", None),
            P("tensor", None),
        ),
        out_specs=P(("groups", "tensor"), None),
        check_vma=False,
    )
```

profile of v0, /device:TPU:0, one launch (start us, length us, event | category | flops | bytes accessed | tf_op | source)
XLA Modules:
  0.0 137.5 jit_solution(9280711550481725237)
XLA Ops:
  0.0 0.9 fusion.1
  0.9 0.9 fusion.4
  1.8 24.6 %all-gather = bf16[16,2,8192]{2,1,0:T(2,128)(2,1)S(1)} all-gather(bf16[1,2,8192]{2,1,0:T(2,128)(2,1)S(1)} %fusion.4), channel_id=1, replica_groups=mesh['groups'=2,'tensor'=16] {'tensor'}, dimensions={0}, use_global_device_ids=true | all-gather | bytes 557056 | tf_op jit(solution)/shard_map/all_gather | solution.py:40
  26.4 0.2 reshape.31
  26.6 0.7 select_convert_fusion.2
  27.4 0.1 copy.17
  27.5 9.8 %bitcast_multiply_fusion.2 = bf16[8192,1024]{1,0:T(8,128)(2,1)S(1)} fusion(bf16[8192,1024]{1,0:T(8,128)(2,1)} %param.15, bf16[128,1024]{1,0:T(8,128)(2,1)S(1)} %copy.17), kind=kLoop, calls=%fused_computation.3 | loop fusion | flops 8388608 | bytes 33816576 | tf_op jit(solution)/shard_map/mul | solution.py:12
  37.4 0.0 copy-start
  37.4 0.0 copy-start.1
  37.4 3.0 %fusion.5 = f32[32,1024]{1,0:T(8,128)S(1)} fusion(bf16[32,8192]{1,0:T(8,128)(2,1)S(1)} %reshape.31, bf16[8192,1024]{1,0:T(8,128)(2,1)S(1)} %bitcast_multiply_fusion.2), kind=kOutput, calls=%fused_computation.19 | convolution fusion | flops 536870912 | bytes 17432576 | tf_op jit(solution)/shard_map/dot_general | solution.py:41
  40.4 0.0 copy-done
  40.4 0.0 copy-done.1
  40.5 0.1 copy.18
  40.6 9.8 %bitcast_multiply_fusion.1 = bf16[8192,1024]{1,0:T(8,128)(2,1)S(1)} fusion(bf16[8192,1024]{1,0:T(8,128)(2,1)} %param.18, bf16[128,1024]{1,0:T(8,128)(2,1)S(1)} %copy.18), kind=kLoop, calls=%fused_computation.2 | loop fusion | flops 8388608 | bytes 33816576 | tf_op jit(solution)/shard_map/mul | solution.py:12
  50.5 0.0 copy-start.4
  50.5 0.0 copy-start.2
  50.5 0.0 copy-start.3
  50.5 3.0 %fusion = bf16[32,1024]{1,0:T(8,128)(2,1)S(1)} fusion(bf16[32,8192]{1,0:T(8,128)(2,1)S(1)} %reshape.31, bf16[8192,1024]{1,0:T(8,128)(2,1)S(1)} %bitcast_multiply_fusion.1, f32[32,1024]{1,0:T(8,128)S(1)} %fusion.5), kind=kOutput, calls=%fused_computation.5 | convolution fusion | flops 537067520 | bytes 17498112 | tf_op jit(solution)/shard_map/dot_general | solution.py:42
  53.5 0.0 copy-done.4
  53.6 0.6 gather_fusion
  54.2 0.0 copy-done.2
  54.2 0.0 copy-done.3
  54.2 0.3 broadcast_in_dim.28
  54.6 0.5 mul.80
  55.0 8.0 %bitcast_multiply_fusion = bf16[1024,8192]{1,0:T(8,128)(2,1)S(1)} fusion(bf16[1024,8192]{1,0:T(8,128)(2,1)} %param.21, bf16[16,8192]{1,0:T(8,128)(2,1)S(1)} %mul.80), kind=kLoop, calls=%fused_computation.1 | loop fusion | flops 8388608 | bytes 33816576 | tf_op jit(solution)/shard_map/mul | solution.py:12
  63.1 0.0 copy-start.5
  63.1 3.0 %fusion.6 = f32[32,8192]{1,0:T(8,128)S(1)} fusion(bf16[32,1024]{1,0:T(8,128)(2,1)S(1)} %gather_fusion, bf16[1024,8192]{1,0:T(8,128)(2,1)S(1)} %bitcast_multiply_fusion), kind=kOutput, calls=%fused_computation.20 | convolution fusion | flops 536870912 | bytes 17891328 | tf_op jit(solution)/shard_map/dot_general | solution.py:44
  66.1 69.5 %all-reduce.2 = bf16[32,8192]{1,0:T(8,128)(2,1)S(1)} all-reduce(f32[32,8192]{1,0:T(8,128)S(1)} %fusion.6), channel_id=2, replica_groups=mesh['groups'=2,'tensor'=16] {'tensor'}, use_global_device_ids=true, to_apply=%region_1.2.clone | all-reduce | flops 262144 | bytes 1572864
  135.6 0.0 copy-done.5
  135.6 0.6 dynamic-slice
  136.8 0.7 dynamic-slice_convert_fusion
  (7 shorter events, 0.1 us)
Async XLA Ops:
  37.4 3.0 %copy-start = (s32[128,16]{0,1:T(8,128)S(1)}, s32[128,16]{0,1:T(8,128)}, u32[]{:S(2)}) copy-start(s32[128,16]{0,1:T(8,128)} %param.20) | copy-start | bytes 24580
  37.4 3.0 %copy-start.1 = (s32[128,16]{0,1:T(8,128)S(1)}, s32[128,16]{0,1:T(8,128)}, u32[]{:S(2)}) copy-start(s32[128,16]{0,1:T(8,128)} %param.19) | copy-start | bytes 24580
  50.5 3.1 %copy-start.4 = (s32[32]{0:T(128)S(1)}, s32[32]{0:T(128)}, u32[]{:S(2)}) copy-start(s32[32]{0:T(128)} %param.14) | copy-start | bytes 388
  50.5 3.7 %copy-start.2 = (s32[16,128]{1,0:T(8,128)S(1)}, s32[16,128]{1,0:T(8,128)}, u32[]{:S(2)}) copy-start(s32[16,128]{1,0:T(8,128)} %param.23) | copy-start | bytes 24580
  50.5 3.7 %copy-start.3 = (s32[16,128]{1,0:T(8,128)S(1)}, s32[16,128]{1,0:T(8,128)}, u32[]{:S(2)}) copy-start(s32[16,128]{1,0:T(8,128)} %param.22) | copy-start | bytes 24580
  63.1 72.5 %copy-start.5 = (u32[32]{0:T(128)S(1)}, u32[32]{0:T(128)}, u32[]{:S(2)}) copy-start(u32[32]{0:T(128)} %constant.22) | copy-start | bytes 388
where the time goes:
time: 138 us
  blocking collectives  94.1 us (68%)
  other arithmetic  30.2 us (22%)
  matrix products  9.04 us (7%)
  local copies, waits for them, and re-layouts  3.27 us (2%)
    unnamed x1, blocking collectives  69.5 us
    mul x3, other arithmetic, scaled(): blocks = weight.reshape(brow, rows // brow, cols) * widened[:, None, :]  27.6 us
    all_gather x1, blocking collectives, body(): everything = lax.all_gather(normed, 'tensor', axis=0, tiled=True)  24.6 us
    dot_general x1, matrix products, body(): up = jnp.dot(everything, up_scaled, preferred_element_type=jnp.float32)  3.04 us
    dot_general x1, matrix products, body(): gate = jnp.dot(everything, gate_scaled, preferred_element_type=jnp.float32)  3.02 us
    dot_general x1, matrix products, body(): jnp.dot(hidden[token_order], down_scaled, preferred_element_type=jnp.floa...  2.98 us

commit v1 on v0

v1 whole, which is shorter than its diff:
```python
import functools

import jax
import jax.numpy as jnp
from jax import lax
from jax.experimental import pallas as pl
from jax.experimental.pallas import tpu as pltpu
from jax.sharding import PartitionSpec as P

BF = jnp.bfloat16
F32 = jnp.float32
CORES = 2
QG = 4
QR = 4
TILE = 16


def grid_of(n):
    chips = n // CORES
    x = 1
    while (2 * x) * (2 * x) < chips:
        x *= 2
    return chips // x, x


def log2(v):
    return v.bit_length() - 1


def iota(shape, dim):
    return lax.broadcasted_iota(jnp.int32, shape, dim)


def factor(keep, expo):
    power = jnp.where(expo == 0, 1.0, jnp.where(expo > 0, 2.0, 0.5))
    return jnp.where(keep > 0, power, 0.0).astype(F32).astype(BF)


def scale_rows(w, fac, side):
    n = w.shape[0] // side
    cols = w.shape[1]
    parts = []
    for j in range(n):
        row = jnp.broadcast_to(fac[j : j + 1, :], (TILE, cols)).astype(BF)
        block = w[j * side : (j + 1) * side, :].reshape(side // TILE, TILE, cols)
        parts.append((block * row[None]).reshape(side, cols))
    return parts[0] if n == 1 else jnp.concatenate(parts, axis=0)


def kernel(
    Z, X,
    tok_h, gain_h, order_h, gw_h, gk_h, ge_h, uw_h, uk_h, ue_h, dw_h, dk_h, de_h,
    out_ref,
    tok, gain, order, gw, gk, ge, uw, uk, ue, dw, dk, de,
    gfac, ufac, dfac, gbuf, lhs, accg, accu, hid,
    part, csend, crecv, ybuf, xsend, xrecv, zbuf, zrecv,
    small_sem, g_sem, u_sem, d_sem,
    gz_s, gz_r, gx_s, gx_r, gc_s, gc_r,
    rc_s, rc_r, rx_s, rx_r, rz_s, rz_r,
):
    C = CORES
    R, D = tok.shape
    F = gw.shape[1]
    T = C * X * Z * R
    G = TILE // R
    side = D // gk.shape[1]
    KCH = D // QG
    PL = KCH // G
    NC = D // QR
    NCG = NC // G

    me = lax.axis_index("tensor")
    mc = lax.rem(me, C)
    mx = lax.rem(lax.div(me, C), X)
    mz = lax.div(me, C * X)

    def dev(z, x, c):
        return {"tensor": (z * X + x) * C + c}

    def zpeer(d):
        return dev(lax.rem(mz + d, Z), mx, mc)

    def xpeer(d):
        return dev(mz, lax.rem(mx + d, X), mc)

    cpeer = dev(mz, mx, 1 - mc)
    MESH = pl.DeviceIdType.MESH

    barrier = pltpu.get_barrier_semaphore()
    for d in range(1, Z):
        pl.semaphore_signal(barrier, inc=1, device_id=zpeer(d), device_id_type=MESH)
    for d in range(1, X):
        pl.semaphore_signal(barrier, inc=1, device_id=xpeer(d), device_id_type=MESH)
    pl.semaphore_signal(barrier, inc=1, device_id=cpeer, device_id_type=MESH)

    smalls = []
    for i, (a, b) in enumerate(
        ((tok_h, tok), (gain_h, gain), (order_h, order), (gk_h, gk), (ge_h, ge),
         (uk_h, uk), (ue_h, ue), (dk_h, dk), (de_h, de))
    ):
        cp = pltpu.make_async_copy(a, b, small_sem.at[i])
        cp.start()
        smalls.append(cp)
    gcp, ucp, dcp = [], [], []
    for q in range(QG):
        rows = pl.ds(q * KCH, KCH)
        gcp.append(pltpu.make_async_copy(gw_h.at[rows], gw.at[rows], g_sem.at[q]))
        ucp.append(pltpu.make_async_copy(uw_h.at[rows], uw.at[rows], u_sem.at[q]))
        gcp[-1].start()
        ucp[-1].start()
    for q in range(QR):
        cols = pl.ds(q * NC, NC)
        dcp.append(pltpu.make_async_copy(dw_h.at[:, cols], dw.at[:, cols], d_sem.at[q]))
        dcp[-1].start()

    smalls[0].wait()
    smalls[1].wait()
    values = tok[...].astype(F32)
    meansq = jnp.sum(values * values, axis=-1, keepdims=True) * (1.0 / D)
    normed = values * lax.rsqrt(meansq + 1e-05) * gain[...]
    for q in range(QG):
        rowid = iota((TILE, PL), 0)
        piece = jnp.zeros((TILE, PL), F32)
        for g in range(G):
            for i in range(R):
                lo = q * KCH + g * PL
                src = jnp.broadcast_to(normed[i : i + 1, lo : lo + PL], (TILE, PL))
                piece = jnp.where(rowid == g * R + i, src, piece)
        gbuf[q, mc, mx, mz] = piece.astype(BF)

    pl.semaphore_wait(barrier, Z + X - 1)

    def remote(src, dst, s, r, to):
        return pltpu.make_async_remote_copy(
            src_ref=src, dst_ref=dst, send_sem=s, recv_sem=r, device_id=to, device_id_type=MESH
        )

    gz, gx, gc = {}, {}, {}
    for q in range(QG):
        for d in range(1, Z):
            ref = gbuf.at[q, mc, mx, mz]
            gz[q, d] = remote(ref, ref, gz_s.at[q, d - 1], gz_r.at[q, d - 1], zpeer(d))
            gz[q, d].start()

    for s in smalls[2:]:
        s.wait()
    spread = (iota((F // side, F), 1) >> log2(side)) == iota((F // side, F), 0)
    spread = spread.astype(F32).astype(BF)
    outer = (((0,), (0,)), ((), ()))
    gfac[...] = lax.dot_general(factor(gk[...], ge[...]), spread, outer, preferred_element_type=F32)
    ufac[...] = lax.dot_general(factor(uk[...], ue[...]), spread, outer, preferred_element_type=F32)

    def gather_x(q):
        for d in range(1, Z):
            gz[q, d].wait_recv()
        for d in range(1, X):
            ref = gbuf.at[q, mc, mx]
            gx[q, d] = remote(ref, ref, gx_s.at[q, d - 1], gx_r.at[q, d - 1], xpeer(d))
            gx[q, d].start()

    def gather_c(q):
        for d in range(1, X):
            gx[q, d].wait_recv()
        ref = gbuf.at[q, mc]
        gc[q] = remote(ref, ref, gc_s.at[q], gc_r.at[q], cpeer)
        gc[q].start()

    for step in range(QG + 1):
        if step < QG:
            gather_x(step)
        if step >= 1:
            gather_c(step - 1)

    dk_fac = factor(dk[...], de[...])
    for q in range(QR):
        wide = (D // side, NC)
        sel = ((iota(wide, 1) + q * NC) >> log2(side)) == iota(wide, 0)
        dfac[:, q * NC : (q + 1) * NC] = jnp.dot(dk_fac, sel.astype(F32).astype(BF), preferred_element_type=F32)

    def token_of(r):
        i = r & (R - 1)
        z = (r >> log2(R)) & (Z - 1)
        x = (r >> log2(R * Z)) & (X - 1)
        c = r >> log2(R * Z * X)
        return ((z * X + x) * C + c) * R + i

    ones = lambda m: m.astype(F32).astype(BF)
    tt = (T, T)
    s_in = ones(token_of(iota(tt, 0)) == iota(tt, 1))
    s_out = ones(token_of(iota(tt, 1)) == iota(tt, 0))
    mt = ones(iota(tt, 0) == jnp.broadcast_to(order[...], tt))
    pt = jnp.dot(s_in, mt, preferred_element_type=F32).astype(BF)
    pt = jnp.dot(pt, s_out, preferred_element_type=F32)
    pick = pt.T.astype(BF)

    nd = TILE * TILE
    o, s = iota((nd, nd), 0), iota((nd, nd), 1)
    og, od, oi = o >> log2(TILE * R), (o >> log2(R)) & (TILE - 1), o & (R - 1)
    perm = ones(s == od * TILE + og * R + oi)

    KS = 8 * side
    for q in range(QG):
        gc[q].wait_recv()
        rows = gbuf[q].reshape(C * X * Z * TILE, PL)
        for b in range(C * X * Z // TILE):
            y = jnp.dot(perm, rows[b * nd : (b + 1) * nd], preferred_element_type=F32).astype(BF)
            n = TILE * R
            for g in range(G):
                lhs[q, b * n : (b + 1) * n, g * PL : (g + 1) * PL] = y[g * n : (g + 1) * n]
        gcp[q].wait()
        ucp[q].wait()
        if q == 0:
            accg[...] = jnp.zeros_like(accg)
            accu[...] = jnp.zeros_like(accu)

        def gate_up(s, carry, q=q):
            ks = pl.ds(pl.multiple_of(q * KCH + s * KS, KS), KS)
            fs = pl.ds(pl.multiple_of((q * KCH + s * KS) // side, 8), 8)
            left = lhs[q, :, pl.ds(pl.multiple_of(s * KS, KS), KS)]
            wg = scale_rows(gw[ks, :], gfac[fs, :], side)
            accg[...] += jnp.dot(left, wg, preferred_element_type=F32)
            wu = scale_rows(uw[ks, :], ufac[fs, :], side)
            accu[...] += jnp.dot(left, wu, preferred_element_type=F32)
            return carry

        lax.fori_loop(0, KCH // KS, gate_up, 0)

    gate = accg[...]
    hidden = (gate / (1.0 + jnp.exp(-gate)) * accu[...]).astype(BF)
    hid[...] = jnp.dot(pick, hidden, preferred_element_type=F32).astype(BF)

    half = X * Z * R
    fold = max(1, TILE // (Z * R))
    zr = Z * R
    zn = G * zr
    o, s = iota((zn, zn), 0), iota((zn, zn), 1)
    oz, og, oi = o >> log2(TILE), (o >> log2(R)) & (G - 1), o & (R - 1)
    perm_z = ones(s == og * zr + oz * R + oi)

    rc, rx, rz = {}, {}, {}

    def folded(v):
        w = NC // fold
        return jnp.concatenate([v[:, h * w : (h + 1) * w] for h in range(fold)], axis=0) if fold > 1 else v

    NS = 512

    def down(q):
        dcp[q].wait()

        def tile(n, carry):
            cols = pl.ds(pl.multiple_of(q * NC + n * NS, NS), NS)
            w = scale_rows(dw[:, cols], dfac[:, cols], side)
            y = jnp.dot(hid[...], w, preferred_element_type=F32)
            part[q, :, :, pl.ds(pl.multiple_of(n * NS, NS), NS)] = y.reshape(C, half, NS)
            return carry

        lax.fori_loop(0, NC // NS, tile, 0)
        csend[q] = part[q, 1 - mc].astype(BF)
        rc[q] = remote(csend.at[q], crecv.at[q], rc_s.at[q], rc_r.at[q], cpeer)
        rc[q].start()

    def reduce_x(q):
        rc[q].wait_recv()
        ybuf[q] = (part[q, mc] + crecv[q].astype(F32)).reshape(X, zr, NC)
        for d in range(1, X):
            xsend[q, d - 1] = folded(ybuf[q, lax.rem(mx + d, X)]).astype(BF)
            rx[q, d] = remote(
                xsend.at[q, d - 1], xrecv.at[q, d - 1], rx_s.at[q, d - 1], rx_r.at[q, d - 1], xpeer(d)
            )
            rx[q, d].start()

    def reduce_z(q):
        y = folded(ybuf[q, mx])
        for d in range(1, X):
            rx[q, d].wait_recv()
            y = y + xrecv[q, d - 1].astype(F32)
        per = G // fold
        stack = [
            y[(g // per) * zr : (g // per + 1) * zr, (g % per) * NCG : (g % per + 1) * NCG] for g in range(G)
        ]
        stack = jnp.concatenate(stack, axis=0).astype(BF)
        zbuf[q] = jnp.dot(perm_z, stack, preferred_element_type=F32).astype(BF).reshape(Z, TILE, NCG)
        for d in range(1, Z):
            rz[q, d] = remote(
                zbuf.at[q, lax.rem(mz + d, Z)], zrecv.at[q, d - 1],
                rz_s.at[q, d - 1], rz_r.at[q, d - 1], zpeer(d),
            )
            rz[q, d].start()

    def finish(q):
        y = zbuf[q, mz].astype(F32)
        for d in range(1, Z):
            rz[q, d].wait_recv()
            y = y + zrecv[q, d - 1].astype(F32)
        for g in range(G):
            for i in range(R):
                lo = q * NC + g * NCG
                out_ref[i : i + 1, lo : lo + NCG] = y[g * R + i : g * R + i + 1]

    for step in range(QR + 3):
        if step < QR:
            down(step)
        if 0 <= step - 1 < QR:
            reduce_x(step - 1)
        if 0 <= step - 2 < QR:
            reduce_z(step - 2)
        if 0 <= step - 3 < QR:
            finish(step - 3)

    for group in (gz, gx, gc, rc, rx, rz):
        for cp in group.values():
            cp.wait_send()


def body(*args):
    tokens, norm_gain, token_order, gw, gk, ge, uw, uk, ue, dw, dk, de = args
    n = lax.axis_size("tensor")
    Z, X = grid_of(n)
    C = CORES
    R, D = tokens.shape
    F = gw.shape[1]
    T = n * R
    assert TILE % R == 0 and n % TILE == 0 and token_order.shape == (T,)
    G = TILE // R
    KCH, NC = D // QG, D // QR
    half, zr = X * Z * R, Z * R
    fold = max(1, TILE // zr)
    gk, ge, uk, ue = gk.T, ge.T, uk.T, ue.T
    side = D // gk.shape[1]
    V = pltpu.VMEM
    dma = pltpu.SemaphoreType.DMA
    scratch = [
        V((R, D), tokens.dtype), V((1, D), F32), V((1, T), jnp.int32),
        V(gw.shape, BF), V(gk.shape, jnp.int32), V(ge.shape, jnp.int32),
        V(uw.shape, BF), V(uk.shape, jnp.int32), V(ue.shape, jnp.int32),
        V(dw.shape, BF), V(dk.shape, jnp.int32), V(de.shape, jnp.int32),
        V((D // side, F), F32), V((D // side, F), F32), V((F // side, D), F32),
        V((QG, C, X, Z, TILE, KCH // G), BF),
        V((QG, T, KCH), BF),
        V((T, F), F32), V((T, F), F32), V((T, F), BF),
        V((QR, C, half, NC), F32), V((QR, half, NC), BF), V((QR, half, NC), BF),
        V((QR, X, zr, NC), F32),
        V((QR, X - 1, zr * fold, NC // fold), BF), V((QR, X - 1, zr * fold, NC // fold), BF),
        V((QR, Z, TILE, NC // G), BF), V((QR, Z - 1, TILE, NC // G), BF),
        dma((9,)), dma((QG,)), dma((QG,)), dma((QR,)),
        dma((QG, Z - 1)), dma((QG, Z - 1)), dma((QG, X - 1)), dma((QG, X - 1)), dma((QG,)), dma((QG,)),
        dma((QR,)), dma((QR,)), dma((QR, X - 1)), dma((QR, X - 1)), dma((QR, Z - 1)), dma((QR, Z - 1)),
    ]
    out = pl.pallas_call(
        functools.partial(kernel, Z, X),
        out_shape=jax.ShapeDtypeStruct((R, D), F32),
        in_specs=[pl.BlockSpec(memory_space=pl.ANY)] * 12,
        out_specs=pl.BlockSpec(memory_space=pltpu.VMEM),
        scratch_shapes=scratch,
        compiler_params=pltpu.CompilerParams(
            collective_id=0, has_side_effects=True, vmem_limit_bytes=60 * 1024 * 1024
        ),
        cost_estimate=pl.CostEstimate(
            flops=6 * T * D * F, bytes_accessed=6 * D * F, transcendentals=T * F
        ),
    )(tokens, norm_gain.reshape(1, D), token_order.reshape(1, T), gw, gk, ge, uw, uk, ue, dw, dk, de)
    return out.astype(BF)


def solution(mesh):
    return jax.shard_map(
        body,
        mesh=mesh,
        in_specs=(
            P(("groups", "tensor"), None),
            P(),
            P("groups"),
            P(None, "tensor"),
            P(None, "tensor"),
            P(None, "tensor"),
            P(None, "tensor"),
            P(None, "tensor"),
            P(None, "tensor"),
            P("tensor", None),
            P("tensor", None),
            P("tensor", None),
        ),
        out_specs=P(("groups", "tensor"), None),
        check_vma=False,
    )
```

time: 138 us -> 50.9 us (0.37)
  blocking collectives: 94.1 us -> 0 us
  Pallas kernels: 0 us -> 49.2 us
  other arithmetic: 30.2 us -> 1.48 us
  matrix products: 9.04 us -> 0 us
  local copies, waits for them, and re-layouts: 3.27 us -> 0 us
    unnamed x1 -> x0, blocking collectives: 69.5 us -> none
    pallas_call x0 -> x1, Pallas kernels: none -> 49.2 us  [body(): pl.pallas_call(functools.partial(kernel, Z, X), out_shape=jax.ShapeDtypeS...]
    mul x3 -> x0, other arithmetic: 27.6 us -> none  [scaled(): blocks = weight.reshape(brow, rows // brow, cols) * widened[:, None, :]]
    all_gather x1 -> x0, blocking collectives: 24.6 us -> none  [body(): everything = lax.all_gather(normed, 'tensor', axis=0, tiled=True)]
    dot_general x3 -> x0, matrix products: 9.04 us -> none  [the longest x1 3.04 us: body(): up = jnp.dot(everything, up_scaled, preferred_element_type=jnp.float32)]
where the time goes in v1:
time: 50.9 us; the launch traced here: 50.7 us
  Pallas kernels  49.2 us (97%)
  other arithmetic  1.48 us (3%)
    pallas_call x1, Pallas kernels, body(): pl.pallas_call(functools.partial(kernel, Z, X), out_shape=jax.ShapeDtypeS...  49.2 us
    convert_element_type x1, other arithmetic, body(): return out.astype(BF)  1.48 us

profile of v1, /device:TPU:0, one launch (start us, length us, event | category | flops | bytes accessed | tf_op | source)
XLA Modules:
  0.0 50.7 jit_solution(12819698590294077005)
XLA Ops:
  0.0 49.2 %shard_map.118 = f32[2,8192]{1,0:T(2,128)} custom-call(bf16[2,8192]{1,0:T(2,128)(2,1)} %tok_h.1, f32[1,8192]{1,0:T(1,128)} %bitcast.6, s32[1,32]{1,0:T(1,128)} %bitcast.11, bf16[8192,1024]{1,0:T(8,128)(2,1)} %gw_h.1, s32[16,128]{1,0:T(8,128)} %bitcast.7, s32[16,128]{1,0:T(8,128)} %bitcast.8, bf16[8192,1024]{1,0:T(8,128)(2,1)} %uw_h.1, s32[16,128]{1,0:T(8,128)} %bitcast.9, ...), custom_call_target="tpu_custom_call" | custom-call | flops 1610612736 | bytes 50331648 | tf_op jit(solution)/shard_map/pallas_call | solution.py:350
  49.2 1.5 %convert_element_type.3 = bf16[2,8192]{1,0:T(2,128)(2,1)} convert(f32[2,8192]{1,0:T(2,128)} %shard_map.118) | non-fusion elementwise | flops 16384 | bytes 98304 | tf_op jit(solution)/shard_map/convert_element_type | solution.py:363

commit v2 on v1

--- a/solution.py
+++ b/solution.py
@@ -10,8 +10,8 @@
 BF = jnp.bfloat16
 F32 = jnp.float32
 CORES = 2
-QG = 4
-QR = 4
+QG = 2
+QR = 2
 TILE = 16
 
 
@@ -106,12 +106,12 @@
         rows = pl.ds(q * KCH, KCH)
         gcp.append(pltpu.make_async_copy(gw_h.at[rows], gw.at[rows], g_sem.at[q]))
         ucp.append(pltpu.make_async_copy(uw_h.at[rows], uw.at[rows], u_sem.at[q]))
-        gcp[-1].start()
-        ucp[-1].start()
+        if q == 0:
+            gcp[-1].start()
+            ucp[-1].start()
     for q in range(QR):
         cols = pl.ds(q * NC, NC)
         dcp.append(pltpu.make_async_copy(dw_h.at[:, cols], dw.at[:, cols], d_sem.at[q]))
-        dcp[-1].start()
 
     smalls[0].wait()
     smalls[1].wait()
@@ -168,6 +168,12 @@
     for step in range(QG + 1):
         if step < QG:
             gather_x(step)
+            if step + 1 < QG:
+                gcp[step + 1].start()
+                ucp[step + 1].start()
+            else:
+                for cp in dcp:
+                    cp.start()
         if step >= 1:
             gather_c(step - 1)
 
@@ -223,7 +229,7 @@
             accu[...] += jnp.dot(left, wu, preferred_element_type=F32)
             return carry
 
-        lax.fori_loop(0, KCH // KS, gate_up, 0)
+        lax.fori_loop(0, KCH // KS, gate_up, 0, unroll=4)
 
     gate = accg[...]
     hidden = (gate / (1.0 + jnp.exp(-gate)) * accu[...]).astype(BF)
@@ -255,7 +261,7 @@
             part[q, :, :, pl.ds(pl.multiple_of(n * NS, NS), NS)] = y.reshape(C, half, NS)
             return carry
 
-        lax.fori_loop(0, NC // NS, tile, 0)
+        lax.fori_loop(0, NC // NS, tile, 0, unroll=4)
         csend[q] = part[q, 1 - mc].astype(BF)
         rc[q] = remote(csend.at[q], crecv.at[q], rc_s.at[q], rc_r.at[q], cpeer)
         rc[q].start()

time: 50.9 us -> 35.3 us (0.69)
  Pallas kernels: 49.2 us -> 33.7 us
    pallas_call x1, Pallas kernels: 49.2 us -> 33.7 us  [body(): pl.pallas_call(functools.partial(kernel, Z, X), out_shape=jax.ShapeDtypeS...]
where the time goes in v2:
time: 35.3 us; the launch traced here: 35.1 us
  Pallas kernels  33.7 us (95%)
  other arithmetic  1.48 us (4%)
    pallas_call x1, Pallas kernels, body(): pl.pallas_call(functools.partial(kernel, Z, X), out_shape=jax.ShapeDtypeS...  33.7 us
    convert_element_type x1, other arithmetic, body(): return out.astype(BF)  1.48 us

profile of v2, /device:TPU:0, one launch (start us, length us, event | category | flops | bytes accessed | tf_op | source)
XLA Modules:
  0.0 35.1 jit_solution(1458432816833419370)
XLA Ops:
  0.0 33.7 %shard_map.118 = f32[2,8192]{1,0:T(2,128)} custom-call(bf16[2,8192]{1,0:T(2,128)(2,1)} %tok_h.1, f32[1,8192]{1,0:T(1,128)} %bitcast.6, s32[1,32]{1,0:T(1,128)} %bitcast.11, bf16[8192,1024]{1,0:T(8,128)(2,1)} %gw_h.1, s32[16,128]{1,0:T(8,128)} %bitcast.7, s32[16,128]{1,0:T(8,128)} %bitcast.8, bf16[8192,1024]{1,0:T(8,128)(2,1)} %uw_h.1, s32[16,128]{1,0:T(8,128)} %bitcast.9, ...), custom_call_target="tpu_custom_call" | custom-call | flops 1610612736 | bytes 50331648 | tf_op jit(solution)/shard_map/pallas_call | solution.py:356
  33.7 1.5 %convert_element_type.3 = bf16[2,8192]{1,0:T(2,128)(2,1)} convert(f32[2,8192]{1,0:T(2,128)} %shard_map.118) | non-fusion elementwise | flops 16384 | bytes 98304 | tf_op jit(solution)/shard_map/convert_element_type | solution.py:369
